TPU v7x, 256 devices: a whole 4x4x8 slice. The times are simulated.
256 devices in a mesh: tm: 8 (over y, core), height: 8 (over x, z_hi), heads: 4 (over z_lo).
Axes of the slice: x: 4, y: 4, z: 8 (z_hi: 2, z_lo: 4; z = z_hi * 4 + z_lo), core: 2. Of those that a mesh axis runs over, the one named last changes fastest.
Arguments:
- q_raw: bfloat16 [48, 64, 4, 1536], P('tm', 'height', None, 'heads'), may hold values from -4 to 4
- k_raw: bfloat16 [48, 64, 4, 1536], P('tm', 'height', None, 'heads'), may hold values from -4 to 4
- value_in: bfloat16 [48, 64, 4, 1536], P('tm', 'height', None, 'heads'), may hold values from -6 to 6
- out_grad: bfloat16 [48, 64, 4, 1536], P('tm', 'height', None, 'heads'), may hold values from -6 to 6
- q_gain: float32 [128], replicated, may hold values from 0.3 to 5
- k_gain: float32 [128], replicated, may hold values from 0.3 to 5
Outputs:
- q_grad: bfloat16 [48, 64, 4, 1536], P('tm', 'height', None, 'heads')
- k_grad: bfloat16 [48, 64, 4, 1536], P('tm', 'height', None, 'heads')
- v_grad: bfloat16 [48, 64, 4, 1536], P('tm', 'height', None, 'heads')
- q_gain_grad: float32 [128], replicated
- k_gain_grad: float32 [128], replicated
All inputs are finite; a program needn't handle non-finite values.
Results may differ from a plain program's by a relative error of at most 0.038.
The roundings to bfloat16 on the way count: a program that leaves them out, or rounds other values in their place, can miss the bound.
Values may be sent and summed in bfloat16 or wider, within the bound.
No kernel may reach another device: no remote copies, remote signals or barrier semaphores. Data moves between devices by JAX's collectives and lax.ppermute only.
A program may use at most 64 MiB of HBM per device.

v0:
```python
import functools
import math

import jax
import jax.numpy as jnp
from jax import lax
from jax.experimental import pallas as pl
from jax.experimental.pallas import tpu as pltpu
from jax.sharding import PartitionSpec as P

HEAD_DIM = 128
EPS = 1e-06
MASKED = -1e30
NT = (((1,), (1,)), ((), ()))
NN = (((1,), (0,)), ((), ()))
TN = (((0,), (0,)), ((), ()))
f32 = jnp.float32
bf16 = jnp.bfloat16
COST = pl.CostEstimate(flops=10**6, bytes_accessed=10**5, transcendentals=0)


def dot(a, b, dims):
    return lax.dot_general(a, b, dims, preferred_element_type=f32)


def unit_of(raw):
    values = raw.astype(f32)
    inverse = lax.rsqrt(jnp.mean(values * values, axis=-1, keepdims=True) + EPS)
    return values * inverse, inverse


def head_cols(channels):
    return [slice(at, at + HEAD_DIM) for at in range(0, channels, HEAD_DIM)]


def stack_kernel(raw_ref, other_ref, gain_ref, *refs):
    flat_in, out_ref, flat_out = refs[: len(refs) // 2], refs[len(refs) // 2], refs[len(refs) // 2 + 1 :]
    tokens = out_ref.shape[2]
    for cols in head_cols(raw_ref.shape[-1]):
        unit, _ = unit_of(raw_ref[..., cols].reshape(tokens, HEAD_DIM))
        out_ref[0, 0, :, cols] = (unit * gain_ref[...]).astype(bf16)
        out_ref[0, 1, :, cols] = other_ref[..., cols].reshape(tokens, HEAD_DIM)
        for ref, flat_ref in zip(flat_in, flat_out):
            flat_ref[:, cols] = ref[..., cols].reshape(tokens, HEAD_DIM)


def norm_stack(raw, other, gain, *flat):
    tokens, channels = math.prod(raw.shape[:-1]), raw.shape[-1]
    return pl.pallas_call(
        stack_kernel,
        out_shape=[jax.ShapeDtypeStruct((1, 2, tokens, channels), bf16)]
        + [jax.ShapeDtypeStruct((tokens, channels), bf16) for _ in flat],
        cost_estimate=COST,
        name="norm_stack",
    )(raw, other, gain, *flat)


def fill(tiles, first, second):
    tile = tiles[0].shape[2]
    for i, ref in enumerate(tiles):
        rows = slice(i * tile, (i + 1) * tile)
        first[rows, :] = ref[0, 0]
        second[rows, :] = ref[0, 1]


def norm_back(grad_norm, raw, gain):
    unit, inverse = unit_of(raw)
    g = grad_norm * gain
    inner = jnp.mean(g * unit, axis=-1, keepdims=True)
    return ((g - unit * inner) * inverse).astype(bf16), unit


def query_kernel(scale, q_ref, qg_ref, qgain_ref, kgain_ref, bias_ref, *refs):
    tiles, (qgrad_ref, sums_ref, stats_ref), (keys, values) = refs[:9], refs[9:12], refs[12:]
    _, _, tile, channels = qg_ref.shape
    heads = head_cols(channels)
    fill(tiles, keys, values)
    lane = lax.broadcasted_iota(jnp.int32, (tile, HEAD_DIM), 1)
    columns = jnp.zeros((tile, HEAD_DIM), f32)
    q_terms = k_terms = jnp.zeros((1, HEAD_DIM), f32)
    scores = [
        dot(qg_ref[0, 0, :, cols], keys[:, cols], NT) * scale + bias_ref[...] for cols in heads
    ]
    prob_grads = [dot(qg_ref[0, 1, :, cols], values[:, cols], NT) for cols in heads]
    probs = []
    for h, cols in enumerate(heads):
        highest = jnp.max(scores[h], axis=-1, keepdims=True)
        terms = jnp.exp(scores[h] - highest)
        total = jnp.sum(terms, axis=-1, keepdims=True)
        probs.append(terms * (1.0 / total))
        columns = jnp.where(lane == 2 * h, highest + jnp.log(total), columns)
    outs = [dot(probs[h].astype(bf16), values[:, cols], NN).astype(bf16) for h, cols in enumerate(heads)]
    grads = []
    for h, cols in enumerate(heads):
        products = qg_ref[0, 1, :, cols].astype(f32) * outs[h].astype(f32)
        delta = jnp.sum(products, axis=-1, keepdims=True)
        columns = jnp.where(lane == 2 * h + 1, delta, columns)
        score_grad = (probs[h] * (prob_grads[h] - delta)).astype(bf16)
        grads.append(dot(score_grad, keys[:, cols], NN) * scale)
    for h, cols in enumerate(heads):
        qgrad_ref[:, cols], unit = norm_back(grads[h], q_ref[:, cols], qgain_ref[...])
        qn = qg_ref[0, 0, :, cols].astype(f32)
        q_terms += jnp.sum(grads[h] * unit, axis=0, keepdims=True)
        k_terms += jnp.sum(grads[h] * qn, axis=0, keepdims=True)
    sums_ref[0:1] = q_terms
    sums_ref[1:2] = k_terms / kgain_ref[...]
    stats_ref[...] = columns.T[:8]


def key_kernel(scale, n, bias_ref, *refs):
    stats, queries_in, keys_in = refs[:3], refs[3:6], refs[6 : 6 + n]
    outs, (queries, grads, keys, values) = refs[6 + n : -4], refs[-4:]
    _, _, tile, channels = queries_in[0].shape
    heads = head_cols(channels)
    fill(queries_in, queries, grads)
    fill(keys_in, keys, values)
    rows = jnp.concatenate([ref[...] for ref in stats], axis=1)
    scores = [dot(keys[:, cols], queries[:, cols], NT) * scale for cols in heads]
    prob_grads = [dot(values[:, cols], grads[:, cols], NT) for cols in heads]
    for h, cols in enumerate(heads):
        prob = jnp.exp(scores[h] + (bias_ref[...] - rows[2 * h : 2 * h + 1]))
        value_terms = dot(prob.astype(bf16), grads[:, cols], NN)
        score_grad = (prob * (prob_grads[h] - rows[2 * h + 1 : 2 * h + 2])).astype(bf16)
        key_terms = dot(score_grad, queries[:, cols], NN) * scale
        for i, ref in enumerate(outs):
            part = slice(i * tile, (i + 1) * tile)
            ref[0, 0, :, cols] = key_terms[part].astype(ref.dtype)
            ref[0, 1, :, cols] = value_terms[part].astype(ref.dtype)


def query_side(q, qg, qgain, kgain, bias, tiles, scale):
    _, _, tile, channels = qg.shape
    span = len(tiles) * tile
    qgrad = jax.ShapeDtypeStruct(q.shape, bf16)
    sums = jax.ShapeDtypeStruct((2, HEAD_DIM), f32)
    stats = jax.ShapeDtypeStruct((8, tile), f32)
    return pl.pallas_call(
        functools.partial(query_kernel, scale),
        out_shape=[qgrad, sums, stats],
        scratch_shapes=[
            pltpu.VMEM((span, channels), bf16),
            pltpu.VMEM((span, channels), bf16),
        ],
        compiler_params=pltpu.CompilerParams(vmem_limit_bytes=40 * 2**20),
        cost_estimate=COST,
        name="query_side",
    )(in_vmem(q), qg, qgain, kgain, bias, *map(in_vmem, tiles))


def key_side(bias, stats, queries, keys, types, scale):
    shape = keys[0].shape
    _, _, tile, channels = shape
    held = [pltpu.VMEM((n * tile, channels), bf16) for n in (3, 3, len(keys), len(keys))]
    return pl.pallas_call(
        functools.partial(key_kernel, scale, len(keys)),
        out_shape=[jax.ShapeDtypeStruct(shape, t) for t in types],
        scratch_shapes=held,
        compiler_params=pltpu.CompilerParams(vmem_limit_bytes=40 * 2**20),
        cost_estimate=COST,
        name="key_side",
    )(bias, *stats, *map(in_vmem, queries), *keys)


def finish_kernel(factor, k_ref, gain_ref, own_ref, mate_ref, sums_ref, *outs):
    kgrad_ref, vgrad_ref, *totals = outs
    for i, ref in enumerate(totals):
        ref[...] = sums_ref[i : i + 1] * factor
    part = kgrad_ref.shape[:-1] + (HEAD_DIM,)
    for cols in head_cols(k_ref.shape[-1]):
        total = [own_ref[0, i, :, cols] + mate_ref[0, i, :, cols].astype(f32) for i in range(2)]
        vgrad_ref[..., cols] = total[1].astype(bf16).reshape(part)
        kgrad, _ = norm_back(total[0], k_ref[:, cols], gain_ref[...])
        kgrad_ref[..., cols] = kgrad.reshape(part)


def finish(k, gain, own, mate, sums, shape, factor):
    total = jax.ShapeDtypeStruct((1, HEAD_DIM), f32)
    return pl.pallas_call(
        functools.partial(finish_kernel, factor),
        out_shape=[jax.ShapeDtypeStruct(shape, bf16)] * 2 + [total] * 2,
        cost_estimate=COST,
        name="finish",
    )(in_vmem(k), gain, in_vmem(own), in_vmem(mate), sums)


def in_vmem(x):
    return pltpu.with_memory_space_constraint(x, pltpu.VMEM)


def swapped(x, axis, bits):
    n = lax.axis_size(axis)
    return lax.ppermute(x, axis, [(i, i ^ bits) for i in range(n)])


def swap(x, axis):
    return swapped(x, axis, 1)


def rows_route(n, back=False):
    route = [(i, i + 2 - 4 * (i % 2)) for i in range(n)]
    return [(j, i) if back else (i, j) for i, j in route if 0 <= j < n]


def frames_route(n):
    return [(i, j) for i in range(n) for j in [i - 1 + 2 * (i % 2)] if 0 <= j < n]


def hop(x, back=False):
    return lax.ppermute(x, "height", rows_route(lax.axis_size("height"), back))


def far(x):
    return lax.ppermute(x, "tm", frames_route(lax.axis_size("tm")))


def level(total, axis, other, bits, other_bits):
    if axis == other:
        far = swapped(total, axis, bits ^ other_bits)
    else:
        n, m = lax.axis_size(axis), lax.axis_size(other)
        route = [
            (i * m + j, (i ^ bits) * m + (j ^ other_bits)) for i in range(n) for j in range(m)
        ]
        far = lax.ppermute(total, (axis, other), route)
    return (total + swapped(total, axis, bits)) + (swapped(total, other, other_bits) + far)


def together(steps, like, *args):
    always = lax.optimization_barrier(jnp.bool_(True))
    return lax.cond(always, steps, like, *args)


def frames(kv, qg):
    return swap(kv, "tm"), swap(qg, "tm"), far(kv), far(qg)


def last_levels(sums):
    n_tm, n_h = lax.axis_size("tm"), lax.axis_size("height")
    groups = [
        [t * n_h + r for t in range(a, n_tm, 2) for r in range(b, n_h, 2)]
        for a in range(2)
        for b in range(2)
    ]
    sent = jnp.broadcast_to(sums[None], (len(groups[0]),) + sums.shape)
    got = lax.all_to_all(sent, ("tm", "height"), 0, 0, axis_index_groups=groups)
    return jnp.sum(got, axis=0)


def after(x, first):
    return lax.optimization_barrier((x, first))[0]


def plus(a, b):
    return (a.astype(f32) + b.astype(f32)).astype(bf16)


def outside(axis):
    at, n = lax.axis_index(axis), lax.axis_size(axis)
    return (at == 0) | (at == n - 1)


def mask_bias(tile, rows):
    each = 3 if rows else 1
    slot = lax.broadcasted_iota(jnp.int32, (1, 3 * each * tile), 1) // tile
    gone = outside("tm") & (slot >= 2 * each)
    if rows:
        gone |= outside("height") & (slot % 3 == 2)
    return jnp.where(gone, MASKED, 0.0).astype(f32)


def with_sums(stats, sums):
    return stats.at[6:8, :HEAD_DIM].set(sums)


def shards(q_raw, k_raw, value_in, out_grad, q_gain, k_gain):
    shape = q_raw.shape
    channels = shape[-1]
    tile = math.prod(shape[:-1])
    scale = 1.0 / math.sqrt(HEAD_DIM)
    count = tile * (channels // HEAD_DIM)
    for axis in ("tm", "height", "heads"):
        count *= lax.axis_size(axis)
    qg_gain, kg_gain = q_gain.reshape(1, HEAD_DIM), k_gain.reshape(1, HEAD_DIM)

    (kv,) = norm_stack(k_raw, value_in, kg_gain)
    z = swap(kv, "height")
    qg, q_flat, k_flat = norm_stack(q_raw, out_grad, qg_gain, q_raw, k_raw)
    c0, d0, y0, w0 = together(frames, lambda a, b: (a, b, a, b), kv, qg)
    z, c0, d0, y0, w0 = lax.optimization_barrier((z, c0, d0, y0, w0))
    c1 = swap(z, "tm")
    x, y1 = hop(z), far(z)
    x, y1, c1 = lax.optimization_barrier((x, y1, c1))
    y2, c2 = far(x), swap(x, "tm")
    tiles = [kv, z, x, c0, c1, c2, y0, y1, y2]
    q_out, sums, stats = query_side(
        q_flat, qg, qg_gain, kg_gain, mask_bias(tile, True), tiles, scale
    )

    c_stats = swap(with_sums(stats, sums), "tm")
    sums = sums + c_stats[6:8, :HEAD_DIM]
    y_stats = far(stats)
    sums = level(sums, "heads", "heads", 1, 2)
    near = mask_bias(tile, False), [stats, c_stats, y_stats], [qg, d0, w0]
    (px,) = key_side(*near, [x], [bf16], scale)
    own, pz = key_side(*near, [kv, z], [f32, bf16], scale)
    px, sums = lax.optimization_barrier((px, sums))
    pz = plus(pz, hop(px, True))
    sums = sums + swap(sums, "height")
    pz, sums = lax.optimization_barrier((pz, sums))
    pz = swap(pz, "height")
    sums = together(last_levels, lambda t: t, sums)
    factor = 1.0 / math.sqrt(count)
    k_out, v_out, q_total, k_total = finish(k_flat, kg_gain, own, pz, sums, shape, factor)
    return q_out.reshape(shape), k_out, v_out, q_total.reshape(-1), k_total.reshape(-1)


def solution(mesh):
    split = P("tm", "height", None, "heads")
    return jax.shard_map(
        shards,
        mesh=mesh,
        in_specs=(split, split, split, split, P(), P()),
        out_specs=(split, split, split, P(), P()),
        check_vma=False,
    )
```

profile of v0, /device:TPU:1, one launch (start us, length us, event | category | flops | bytes accessed | tf_op | source)
XLA Modules:
  0.0 89.0 jit_solution(14285691853168394639)
XLA Ops:
  1.9 7.8 %collective-permute-start.4 = (bf16[1,2,192,384]{3,2,1,0:T(8,128)(2,1)S(1)}, bf16[1,2,192,384]{3,2,1,0:T(8,128)(2,1)S(1)}, u32[]{:S(2)}, u32[]{:S(2)}) collective-permute-start(bf16[1,2,192,384]{3,2,1,0:T(8,128)(2,1)S(1)} %norm_stack.3.refs_0_.refs_6_), channel_id=1, source_target_pairs={{0,4},{4,0},{8,12},{12,8},{16,20},{20,16},{24,28},{28,24},{1,5},{5... | collective-permute-start | bytes 884744 | tf_op jit(solution)/shard_map/ppermute | solution.py:192
  9.7 2.1 %norm_stack.2 = (bf16[1,2,192,384]{3,2,1,0:T(8,128)(2,1)S(1)}, bf16[192,384]{1,0:T(8,128)(2,1)}, bf16[192,384]{1,0:T(8,128)(2,1)}) custom-call(bf16[6,8,4,384]{3,2,1,0:T(4,128)(2,1)} %refs_0_.1, bf16[6,8,4,384]{3,2,1,0:T(4,128)(2,1)} %other_ref.2, f32[1,128]{1,0:T(1,128)} %bitcast.7, bf16[6,8,4,384]{3,2,1,0:T(4,128)(2,1)} %refs_0_.1, ...), custom_call_target="tpu_custom_call" | custom-call | flops 1000000 | bytes 100000 | tf_op jit(solution)/shard_map/norm_stack/pallas_call | solution.py:49
  11.8 12.7 %conditional.2 = (bf16[1,2,192,384]{3,2,1,0:T(8,128)(2,1)}, bf16[1,2,192,384]{3,2,1,0:T(8,128)(2,1)}, bf16[1,2,192,384]{3,2,1,0:T(8,128)(2,1)}, bf16[1,2,192,384]{3,2,1,0:T(8,128)(2,1)}) conditional(s32[]{:T(128)} %convert_element_type.13, (bf16[1,2,192,384]{3,2,1,0:T(8,128)(2,1)S(1)}, bf16[1,2,192,384]{3,2,1,0:T(8,128)(2,1)S(1)}) %tuple.30, ...), branch_computations={%region_0.0_spmd, %region_1.0_spmd} | conditional | bytes 4718784 | solution.py:230
  12.8 3.5 %collective-permute-start.2 = (bf16[1,2,192,384]{3,2,1,0:T(8,128)(2,1)S(1)}, bf16[1,2,192,384]{3,2,1,0:T(8,128)(2,1)}, u32[]{:S(2)}, u32[]{:S(2)}) collective-permute-start(bf16[1,2,192,384]{3,2,1,0:T(8,128)(2,1)S(1)} %get-tuple-element.27), channel_id=1, source_target_pairs={{32,64},{64,32},{96,128},{128,96},{160,192},{192,160},{33,65},{65,... | collective-permute-start | bytes 884744 | tf_op jit(solution)/shard_map/cond/branch_1_fun/ppermute | solution.py:213
  16.3 2.0 %collective-permute-start.3 = (bf16[1,2,192,384]{3,2,1,0:T(8,128)(2,1)S(1)}, bf16[1,2,192,384]{3,2,1,0:T(8,128)(2,1)}, u32[]{:S(2)}, u32[]{:S(2)}) collective-permute-start(bf16[1,2,192,384]{3,2,1,0:T(8,128)(2,1)S(1)} %get-tuple-element.28), channel_id=1, source_target_pairs={{32,64},{64,32},{96,128},{128,96},{160,192},{192,160},{33,65},{65,... | collective-permute-start | bytes 884744 | tf_op jit(solution)/shard_map/cond/branch_1_fun/ppermute | solution.py:213
  18.4 2.5 %collective-permute-done.2 = bf16[1,2,192,384]{3,2,1,0:T(8,128)(2,1)} collective-permute-done((bf16[1,2,192,384]{3,2,1,0:T(8,128)(2,1)S(1)}, bf16[1,2,192,384]{3,2,1,0:T(8,128)(2,1)}, u32[]{:S(2)}, u32[]{:S(2)}) %collective-permute-start.2) | collective-permute-done | bytes 294944 | tf_op jit(solution)/shard_map/cond/branch_1_fun/ppermute | solution.py:213
  21.0 3.5 %collective-permute-done.3 = bf16[1,2,192,384]{3,2,1,0:T(8,128)(2,1)} collective-permute-done((bf16[1,2,192,384]{3,2,1,0:T(8,128)(2,1)S(1)}, bf16[1,2,192,384]{3,2,1,0:T(8,128)(2,1)}, u32[]{:S(2)}, u32[]{:S(2)}) %collective-permute-start.3) | collective-permute-done | bytes 294944 | tf_op jit(solution)/shard_map/cond/branch_1_fun/ppermute | solution.py:213
  24.5 3.3 %collective-permute-start.5 = (bf16[1,2,192,384]{3,2,1,0:T(8,128)(2,1)S(1)}, bf16[1,2,192,384]{3,2,1,0:T(8,128)(2,1)S(1)}, u32[]{:S(2)}, u32[]{:S(2)}) collective-permute-start(bf16[1,2,192,384]{3,2,1,0:T(8,128)(2,1)S(1)} %collective-permute-done.4.refs_1_.refs_7_), channel_id=1, source_target_pairs={{0,8},{8,16},{12,4},{16,24},{20,12},{28,20},{1,9},{9,17},{13,5},{1... | collective-permute-start | bytes 884744 | tf_op jit(solution)/shard_map/ppermute | solution.py:209
  27.8 3.2 %collective-permute-start.6 = (bf16[1,2,192,384]{3,2,1,0:T(8,128)(2,1)S(1)}, bf16[1,2,192,384]{3,2,1,0:T(8,128)(2,1)S(1)}, u32[]{:S(2)}, u32[]{:S(2)}) collective-permute-start(bf16[1,2,192,384]{3,2,1,0:T(8,128)(2,1)S(1)} %collective-permute-done.4.refs_1_.refs_7_), channel_id=1, source_target_pairs={{32,64},{64,32},{96,128},{128,96},{160,192},{192,160},{33,65},{65,... | collective-permute-start | bytes 884744 | tf_op jit(solution)/shard_map/ppermute | solution.py:213
  31.4 4.4 %collective-permute-done.6.refs_7_ = bf16[1,2,192,384]{3,2,1,0:T(8,128)(2,1)S(1)} collective-permute-done((bf16[1,2,192,384]{3,2,1,0:T(8,128)(2,1)S(1)}, bf16[1,2,192,384]{3,2,1,0:T(8,128)(2,1)S(1)}, u32[]{:S(2)}, u32[]{:S(2)}) %collective-permute-start.6) | collective-permute-done | bytes 294944 | tf_op jit(solution)/shard_map/ppermute | solution.py:213
  35.9 3.4 %collective-permute-start.9 = (bf16[1,2,192,384]{3,2,1,0:T(8,128)(2,1)S(1)}, bf16[1,2,192,384]{3,2,1,0:T(8,128)(2,1)S(1)}, u32[]{:S(2)}, u32[]{:S(2)}) collective-permute-start(bf16[1,2,192,384]{3,2,1,0:T(8,128)(2,1)S(1)} %collective-permute-done.5.refs_2_.refs_6_), channel_id=1, source_target_pairs={{32,64},{64,32},{96,128},{128,96},{160,192},{192,160},{33,65},{65,... | collective-permute-start | bytes 884744 | tf_op jit(solution)/shard_map/ppermute | solution.py:213
  39.4 4.5 %collective-permute-done.9.refs_8_ = bf16[1,2,192,384]{3,2,1,0:T(8,128)(2,1)S(1)} collective-permute-done((bf16[1,2,192,384]{3,2,1,0:T(8,128)(2,1)S(1)}, bf16[1,2,192,384]{3,2,1,0:T(8,128)(2,1)S(1)}, u32[]{:S(2)}, u32[]{:S(2)}) %collective-permute-start.9) | collective-permute-done | bytes 294944 | tf_op jit(solution)/shard_map/ppermute | solution.py:213
  43.9 4.5 %query_side.1 = (bf16[192,384]{1,0:T(8,128)(2,1)S(1)}, f32[2,128]{1,0:T(2,128)S(1)}, f32[8,192]{1,0:T(8,128)S(1)}) custom-call(bf16[192,384]{1,0:T(8,128)(2,1)S(1)} %copy-done.1, bf16[1,2,192,384]{3,2,1,0:T(8,128)(2,1)S(1)} %get-tuple-element.63.qg_ref.refs_3_, f32[1,128]{1,0:T(1,128)S(1)} %bitcast.8, f32[1,128]{1,0:T(1,128)S(1)} %bitcast.6, ...), custom_call_target="tpu_custom_call" | custom-call | flops 1000000 | bytes 100000 | tf_op jit(solution)/shard_map/query_side/pallas_call | solution.py:137
  48.5 3.7 %collective-permute-start.11 = (f32[8,192]{1,0:T(8,128)S(1)}, f32[8,192]{1,0:T(8,128)S(1)}, u32[]{:S(2)}, u32[]{:S(2)}) collective-permute-start(f32[8,192]{1,0:T(8,128)S(1)} %get-tuple-element.76.refs_0_), channel_id=1, source_target_pairs={{32,64},{64,32},{96,128},{128,96},{160,192},{192,160},{33,65},{65,... | collective-permute-start | bytes 18440 | tf_op jit(solution)/shard_map/ppermute | solution.py:213
  54.3 1.6 %collective-permute-start.14 = (f32[2,128]{1,0:T(2,128)S(1)}, f32[2,128]{1,0:T(2,128)S(1)}, u32[]{:S(2)}, u32[]{:S(2)}) collective-permute-start(f32[2,128]{1,0:T(2,128)S(1)} %slice_add_fusion), channel_id=1, source_target_pairs={{0,3},{1,2},{2,1},{3,0},{4,7},{5,6},{6,5},{7,4},{8,11},{9,10},{10,... | collective-permute-start | bytes 3080 | tf_op jit(solution)/shard_map/ppermute | solution.py:192
  55.9 2.2 %key_side.3 = bf16[1,2,192,384]{3,2,1,0:T(8,128)(2,1)S(1)} custom-call(f32[1,576]{1,0:T(1,128)S(1)} %and_select_fusion.2.bias_ref, f32[8,192]{1,0:T(8,128)S(1)} %get-tuple-element.76.refs_0_, f32[8,192]{1,0:T(8,128)S(1)} %collective-permute-done.10.refs_1_, f32[8,192]{1,0:T(8,128)S(1)} %collective-permute-done.11.refs_2_, ...), custom_call_target="tpu_custom_call" | custom-call | flops 1000000 | bytes 100000 | tf_op jit(solution)/shard_map/key_side/pallas_call | solution.py:154
  58.5 1.3 %collective-permute-start.15 = (bf16[1,2,192,384]{3,2,1,0:T(8,128)(2,1)S(1)}, bf16[1,2,192,384]{3,2,1,0:T(8,128)(2,1)S(1)}, u32[]{:S(2)}, u32[]{:S(2)}) collective-permute-start(bf16[1,2,192,384]{3,2,1,0:T(8,128)(2,1)S(1)} %key_side.3), channel_id=1, source_target_pairs={{8,0},{16,8},{4,12},{24,16},{12,20},{20,28},{9,1},{17,9},{5,13},{2... | collective-permute-start | bytes 884744 | tf_op jit(solution)/shard_map/ppermute | solution.py:209
  59.8 5.2 %collective-permute-start.16 = (f32[2,128]{1,0:T(2,128)S(1)}, f32[2,128]{1,0:T(2,128)S(1)}, u32[]{:S(2)}, u32[]{:S(2)}) collective-permute-start(f32[2,128]{1,0:T(2,128)S(1)} %add_add_fusion), channel_id=1, source_target_pairs={{0,4},{4,0},{8,12},{12,8},{16,20},{20,16},{24,28},{28,24},{1,5},{5... | collective-permute-start | bytes 3080 | tf_op jit(solution)/shard_map/ppermute | solution.py:192
  65.0 3.0 %key_side.2 = (f32[1,2,192,384]{3,2,1,0:T(8,128)S(1)}, bf16[1,2,192,384]{3,2,1,0:T(8,128)(2,1)S(1)}) custom-call(f32[1,576]{1,0:T(1,128)S(1)} %and_select_fusion.2.bias_ref, f32[8,192]{1,0:T(8,128)S(1)} %get-tuple-element.76.refs_0_, f32[8,192]{1,0:T(8,128)S(1)} %collective-permute-done.10.refs_1_, f32[8,192]{1,0:T(8,128)S(1)} %collective-permute-done.11.refs_2_, ...), custom_call_target="tpu_custom_call" | custom-call | flops 1000000 | bytes 100000 | tf_op jit(solution)/shard_map/key_side/pallas_call | solution.py:154
  68.7 2.8 %collective-permute-start.17 = (bf16[1,2,192,384]{3,2,1,0:T(8,128)(2,1)S(1)}, bf16[1,2,192,384]{3,2,1,0:T(8,128)(2,1)S(1)}, u32[]{:S(2)}, u32[]{:S(2)}) collective-permute-start(bf16[1,2,192,384]{3,2,1,0:T(8,128)(2,1)S(1)} %add_convert_fusion), channel_id=1, source_target_pairs={{0,4},{4,0},{8,12},{12,8},{16,20},{20,16},{24,28},{28,24},{1,5},{5... | collective-permute-start | bytes 884744 | tf_op jit(solution)/shard_map/ppermute | solution.py:192
  72.2 12.2 %conditional.3 = (f32[2,128]{1,0:T(2,128)S(1)}) conditional(s32[]{:T(128)} %convert_element_type.13, f32[2,128]{1,0:T(2,128)S(1)} %add.58, f32[2,128]{1,0:T(2,128)S(1)} %add.58), branch_computations={%region_2.3_spmd, %region_3.5_spmd} | conditional | flops 3840 | bytes 67596 | solution.py:230
  72.2 12.2 %all_to_all.4 = f32[16,2,128]{2,1,0:T(2,128)S(1)} all-to-all(f32[16,2,128]{2,1,0:T(2,128)S(1)} %broadcast_in_dim.17), channel_id=1, replica_groups={{0,8,16,24,64,72,80,88,128,136,144,152,192,200,208,216},{4,12,20,28,68,..., dimensions={0} | all-to-all | bytes 32768 | tf_op jit(solution)/shard_map/cond/branch_1_fun/all_to_all | solution.py:245
  84.4 2.9 %collective-permute-done.17.mate_ref = bf16[1,2,192,384]{3,2,1,0:T(8,128)(2,1)S(1)} collective-permute-done((bf16[1,2,192,384]{3,2,1,0:T(8,128)(2,1)S(1)}, bf16[1,2,192,384]{3,2,1,0:T(8,128)(2,1)S(1)}, u32[]{:S(2)}, u32[]{:S(2)}) %collective-permute-start.17) | collective-permute-done | bytes 294944 | tf_op jit(solution)/shard_map/ppermute | solution.py:192
  87.3 1.7 %finish.1 = (bf16[6,8,4,384]{3,2,1,0:T(4,128)(2,1)}, bf16[6,8,4,384]{3,2,1,0:T(4,128)(2,1)}, f32[1,128]{1,0:T(1,128)}, f32[1,128]{1,0:T(1,128)}) custom-call(bf16[192,384]{1,0:T(8,128)(2,1)S(1)} %copy-done, f32[1,128]{1,0:T(1,128)} %bitcast.5, f32[1,2,192,384]{3,2,1,0:T(8,128)S(1)} %get-tuple-element.80.own_ref, ...), custom_call_target="tpu_custom_call" | custom-call | flops 1000000 | bytes 100000 | tf_op jit(solution)/shard_map/finish/pallas_call | solution.py:178
  (40 shorter events, 6.6 us)
Async XLA Ops:
  1.9 22.6 %collective-permute-start.4 = (bf16[1,2,192,384]{3,2,1,0:T(8,128)(2,1)S(1)}, bf16[1,2,192,384]{3,2,1,0:T(8,128)(2,1)S(1)}, u32[]{:S(2)}, u32[]{:S(2)}) collective-permute-start(bf16[1,2,192,384]{3,2,1,0:T(8,128)(2,1)S(1)} %norm_stack.3.refs_0_.refs_6_), channel_id=1, source_target_pairs={{0,4},{4,0},{8,12},{12,8},{16,20},{20,16},{24,28},{28,24},{1,5},{5... | collective-permute-start | bytes 884744 | tf_op jit(solution)/shard_map/ppermute | solution.py:192
  11.8 32.1 %copy-start.1 = (bf16[192,384]{1,0:T(8,128)(2,1)S(1)}, bf16[192,384]{1,0:T(8,128)(2,1)}, u32[]{:S(2)}) copy-start(bf16[192,384]{1,0:T(8,128)(2,1)} %get-tuple-element.62.q_ref) | copy-start | bytes 442372
  11.8 6.6 %collective-permute-start = (bf16[1,2,192,384]{3,2,1,0:T(8,128)(2,1)S(1)}, bf16[1,2,192,384]{3,2,1,0:T(8,128)(2,1)}, u32[]{:S(2)}, u32[]{:S(2)}) collective-permute-start(bf16[1,2,192,384]{3,2,1,0:T(8,128)(2,1)S(1)} %get-tuple-element.27), channel_id=1, source_target_pairs={{0,32},{32,0},{64,96},{96,64},{128,160},{160,128},{192,224},{224,1... | collective-permute-start | bytes 884744 | tf_op jit(solution)/shard_map/cond/branch_1_fun/ppermute | solution.py:192
  12.7 5.7 %collective-permute-start.1 = (bf16[1,2,192,384]{3,2,1,0:T(8,128)(2,1)S(1)}, bf16[1,2,192,384]{3,2,1,0:T(8,128)(2,1)}, u32[]{:S(2)}, u32[]{:S(2)}) collective-permute-start(bf16[1,2,192,384]{3,2,1,0:T(8,128)(2,1)S(1)} %get-tuple-element.28), channel_id=1, source_target_pairs={{0,32},{32,0},{64,96},{96,64},{128,160},{160,128},{192,224},{224,1... | collective-permute-start | bytes 884744 | tf_op jit(solution)/shard_map/cond/branch_1_fun/ppermute | solution.py:192
  12.8 8.1 %collective-permute-start.2 = (bf16[1,2,192,384]{3,2,1,0:T(8,128)(2,1)S(1)}, bf16[1,2,192,384]{3,2,1,0:T(8,128)(2,1)}, u32[]{:S(2)}, u32[]{:S(2)}) collective-permute-start(bf16[1,2,192,384]{3,2,1,0:T(8,128)(2,1)S(1)} %get-tuple-element.27), channel_id=1, source_target_pairs={{32,64},{64,32},{96,128},{128,96},{160,192},{192,160},{33,65},{65,... | collective-permute-start | bytes 884744 | tf_op jit(solution)/shard_map/cond/branch_1_fun/ppermute | solution.py:213
  16.3 8.1 %collective-permute-start.3 = (bf16[1,2,192,384]{3,2,1,0:T(8,128)(2,1)S(1)}, bf16[1,2,192,384]{3,2,1,0:T(8,128)(2,1)}, u32[]{:S(2)}, u32[]{:S(2)}) collective-permute-start(bf16[1,2,192,384]{3,2,1,0:T(8,128)(2,1)S(1)} %get-tuple-element.28), channel_id=1, source_target_pairs={{32,64},{64,32},{96,128},{128,96},{160,192},{192,160},{33,65},{65,... | collective-permute-start | bytes 884744 | tf_op jit(solution)/shard_map/cond/branch_1_fun/ppermute | solution.py:213
  24.5 7.0 %collective-permute-start.5 = (bf16[1,2,192,384]{3,2,1,0:T(8,128)(2,1)S(1)}, bf16[1,2,192,384]{3,2,1,0:T(8,128)(2,1)S(1)}, u32[]{:S(2)}, u32[]{:S(2)}) collective-permute-start(bf16[1,2,192,384]{3,2,1,0:T(8,128)(2,1)S(1)} %collective-permute-done.4.refs_1_.refs_7_), channel_id=1, source_target_pairs={{0,8},{8,16},{12,4},{16,24},{20,12},{28,20},{1,9},{9,17},{13,5},{1... | collective-permute-start | bytes 884744 | tf_op jit(solution)/shard_map/ppermute | solution.py:209
  27.8 8.0 %collective-permute-start.6 = (bf16[1,2,192,384]{3,2,1,0:T(8,128)(2,1)S(1)}, bf16[1,2,192,384]{3,2,1,0:T(8,128)(2,1)S(1)}, u32[]{:S(2)}, u32[]{:S(2)}) collective-permute-start(bf16[1,2,192,384]{3,2,1,0:T(8,128)(2,1)S(1)} %collective-permute-done.4.refs_1_.refs_7_), channel_id=1, source_target_pairs={{32,64},{64,32},{96,128},{128,96},{160,192},{192,160},{33,65},{65,... | collective-permute-start | bytes 884744 | tf_op jit(solution)/shard_map/ppermute | solution.py:213
  31.1 4.8 %collective-permute-start.7 = (bf16[1,2,192,384]{3,2,1,0:T(8,128)(2,1)S(1)}, bf16[1,2,192,384]{3,2,1,0:T(8,128)(2,1)S(1)}, u32[]{:S(2)}, u32[]{:S(2)}) collective-permute-start(bf16[1,2,192,384]{3,2,1,0:T(8,128)(2,1)S(1)} %collective-permute-done.4.refs_1_.refs_7_), channel_id=1, source_target_pairs={{0,32},{32,0},{64,96},{96,64},{128,160},{160,128},{192,224},{224,1... | collective-permute-start | bytes 884744 | tf_op jit(solution)/shard_map/ppermute | solution.py:192
  35.9 3.5 %collective-permute-start.8 = (bf16[1,2,192,384]{3,2,1,0:T(8,128)(2,1)S(1)}, bf16[1,2,192,384]{3,2,1,0:T(8,128)(2,1)S(1)}, u32[]{:S(2)}, u32[]{:S(2)}) collective-permute-start(bf16[1,2,192,384]{3,2,1,0:T(8,128)(2,1)S(1)} %collective-permute-done.5.refs_2_.refs_6_), channel_id=1, source_target_pairs={{0,32},{32,0},{64,96},{96,64},{128,160},{160,128},{192,224},{224,1... | collective-permute-start | bytes 884744 | tf_op jit(solution)/shard_map/ppermute | solution.py:192
  35.9 8.0 %collective-permute-start.9 = (bf16[1,2,192,384]{3,2,1,0:T(8,128)(2,1)S(1)}, bf16[1,2,192,384]{3,2,1,0:T(8,128)(2,1)S(1)}, u32[]{:S(2)}, u32[]{:S(2)}) collective-permute-start(bf16[1,2,192,384]{3,2,1,0:T(8,128)(2,1)S(1)} %collective-permute-done.5.refs_2_.refs_6_), channel_id=1, source_target_pairs={{32,64},{64,32},{96,128},{128,96},{160,192},{192,160},{33,65},{65,... | collective-permute-start | bytes 884744 | tf_op jit(solution)/shard_map/ppermute | solution.py:213
  39.3 4.5 %copy-start.2 = (f32[128]{0:T(128)S(1)}, f32[128]{0:T(128)}, u32[]{:S(2)}) copy-start(f32[128]{0:T(128)} %param.17) | copy-start | bytes 1540
  39.4 4.5 %copy-start.3 = (f32[128]{0:T(128)S(1)}, f32[128]{0:T(128)}, u32[]{:S(2)}) copy-start(f32[128]{0:T(128)} %param.16) | copy-start | bytes 1540
  48.4 3.8 %collective-permute-start.10 = (f32[8,192]{1,0:T(8,128)S(1)}, f32[8,192]{1,0:T(8,128)S(1)}, u32[]{:S(2)}, u32[]{:S(2)}) collective-permute-start(f32[8,192]{1,0:T(8,128)S(1)} %constant_dynamic-update-slice_fusion), channel_id=1, source_target_pairs={{0,32},{32,0},{64,96},{96,64},{128,160},{160,128},{192,224},{224,1... | collective-permute-start | bytes 18440 | tf_op jit(solution)/shard_map/ppermute | solution.py:192
  48.5 7.4 %collective-permute-start.11 = (f32[8,192]{1,0:T(8,128)S(1)}, f32[8,192]{1,0:T(8,128)S(1)}, u32[]{:S(2)}, u32[]{:S(2)}) collective-permute-start(f32[8,192]{1,0:T(8,128)S(1)} %get-tuple-element.76.refs_0_), channel_id=1, source_target_pairs={{32,64},{64,32},{96,128},{128,96},{160,192},{192,160},{33,65},{65,... | collective-permute-start | bytes 18440 | tf_op jit(solution)/shard_map/ppermute | solution.py:213
  52.2 5.8 %collective-permute-start.12 = (f32[2,128]{1,0:T(2,128)S(1)}, f32[2,128]{1,0:T(2,128)S(1)}, u32[]{:S(2)}, u32[]{:S(2)}) collective-permute-start(f32[2,128]{1,0:T(2,128)S(1)} %slice_add_fusion), channel_id=1, source_target_pairs={{0,1},{1,0},{2,3},{3,2},{4,5},{5,4},{6,7},{7,6},{8,9},{9,8},{10,11... | collective-permute-start | bytes 3080 | tf_op jit(solution)/shard_map/ppermute | solution.py:192
  53.1 5.0 %collective-permute-start.13 = (f32[2,128]{1,0:T(2,128)S(1)}, f32[2,128]{1,0:T(2,128)S(1)}, u32[]{:S(2)}, u32[]{:S(2)}) collective-permute-start(f32[2,128]{1,0:T(2,128)S(1)} %slice_add_fusion), channel_id=1, source_target_pairs={{0,2},{1,3},{2,0},{3,1},{4,6},{5,7},{6,4},{7,5},{8,10},{9,11},{10,... | collective-permute-start | bytes 3080 | tf_op jit(solution)/shard_map/ppermute | solution.py:192
  54.3 4.2 %collective-permute-start.14 = (f32[2,128]{1,0:T(2,128)S(1)}, f32[2,128]{1,0:T(2,128)S(1)}, u32[]{:S(2)}, u32[]{:S(2)}) collective-permute-start(f32[2,128]{1,0:T(2,128)S(1)} %slice_add_fusion), channel_id=1, source_target_pairs={{0,3},{1,2},{2,1},{3,0},{4,7},{5,6},{6,5},{7,4},{8,11},{9,10},{10,... | collective-permute-start | bytes 3080 | tf_op jit(solution)/shard_map/ppermute | solution.py:192
  58.5 10.1 %collective-permute-start.15 = (bf16[1,2,192,384]{3,2,1,0:T(8,128)(2,1)S(1)}, bf16[1,2,192,384]{3,2,1,0:T(8,128)(2,1)S(1)}, u32[]{:S(2)}, u32[]{:S(2)}) collective-permute-start(bf16[1,2,192,384]{3,2,1,0:T(8,128)(2,1)S(1)} %key_side.3), channel_id=1, source_target_pairs={{8,0},{16,8},{4,12},{24,16},{12,20},{20,28},{9,1},{17,9},{5,13},{2... | collective-permute-start | bytes 884744 | tf_op jit(solution)/shard_map/ppermute | solution.py:209
  59.8 8.3 %collective-permute-start.16 = (f32[2,128]{1,0:T(2,128)S(1)}, f32[2,128]{1,0:T(2,128)S(1)}, u32[]{:S(2)}, u32[]{:S(2)}) collective-permute-start(f32[2,128]{1,0:T(2,128)S(1)} %add_add_fusion), channel_id=1, source_target_pairs={{0,4},{4,0},{8,12},{12,8},{16,20},{20,16},{24,28},{28,24},{1,5},{5... | collective-permute-start | bytes 3080 | tf_op jit(solution)/shard_map/ppermute | solution.py:192
  68.7 18.7 %collective-permute-start.17 = (bf16[1,2,192,384]{3,2,1,0:T(8,128)(2,1)S(1)}, bf16[1,2,192,384]{3,2,1,0:T(8,128)(2,1)S(1)}, u32[]{:S(2)}, u32[]{:S(2)}) collective-permute-start(bf16[1,2,192,384]{3,2,1,0:T(8,128)(2,1)S(1)} %add_convert_fusion), channel_id=1, source_target_pairs={{0,4},{4,0},{8,12},{12,8},{16,20},{20,16},{24,28},{28,24},{1,5},{5... | collective-permute-start | bytes 884744 | tf_op jit(solution)/shard_map/ppermute | solution.py:192
  71.5 15.9 %copy-start = (bf16[192,384]{1,0:T(8,128)(2,1)S(1)}, bf16[192,384]{1,0:T(8,128)(2,1)}, u32[]{:S(2)}) copy-start(bf16[192,384]{1,0:T(8,128)(2,1)} %get-tuple-element.75.k_ref) | copy-start | bytes 442372
where the time goes:
time: 89.4 us; the launch traced here: 89 us
  starting transfers between devices  41.2 us (46%)
  waiting for transfers between devices  19.1 us (21%)
  Pallas kernels  14.7 us (16%)
  blocking collectives  12.2 us (14%)
    ppermute x11, starting transfers between devices, swapped(): return lax.ppermute(x, axis, [(i, i ^ bits) for i in range(n)])  20.7 us
    ppermute x5, starting transfers between devices, far(): return lax.ppermute(x, 'tm', frames_route(lax.axis_size('tm')))  15.9 us
    ppermute x5, waiting for transfers between devices, far(): return lax.ppermute(x, 'tm', frames_route(lax.axis_size('tm')))  15 us
    all_to_all x1, blocking collectives, last_levels(): got = lax.all_to_all(sent, ('tm', 'height'), 0, 0, axis_index_groups=groups)  12.2 us
    pallas_call x2, Pallas kernels, key_side(): pl.pallas_call(functools.partial(key_kernel, scale, len(keys)), out_shape...  5.21 us
    ppermute x2, starting transfers between devices, hop(): return lax.ppermute(x, 'height', rows_route(lax.axis_size('height'), back))  4.59 us
    pallas_call x1, Pallas kernels, query_side(): pl.pallas_call(functools.partial(query_kernel, scale), out_shape=[qgrad,...  4.48 us
    ppermute x11, waiting for transfers between devices, swapped(): return lax.ppermute(x, axis, [(i, i ^ bits) for i in range(n)])  3.32 us
  transfers between devices with their start and end apart: 18, of which 8 were waited for; matrix products, arithmetic and copies ran while one was open for 1% of the time, Pallas kernels for 8%

commit v1 on v0

--- a/solution.py
+++ b/solution.py
@@ -70,8 +70,29 @@
     return ((g - unit * inner) * inverse).astype(bf16), unit
 
 
+def near_kernel(scale, qg_ref, bias_ref, *refs):
+    tiles, (terms_ref, prob_grads_ref, tops_ref, keys, values) = refs[:-5], refs[-5:]
+    _, _, tile, channels = qg_ref.shape
+    fill(tiles, keys, values)
+    lane = lax.broadcasted_iota(jnp.int32, (tile, HEAD_DIM), 1)
+    tops = jnp.zeros((tile, HEAD_DIM), f32)
+    heads = head_cols(channels)
+    scores = [
+        dot(qg_ref[0, 0, :, cols], keys[:, cols], NT) * scale + bias_ref[...] for cols in heads
+    ]
+    for h, cols in enumerate(heads):
+        prob_grads_ref[h] = dot(qg_ref[0, 1, :, cols], values[:, cols], NT)
+        highest = jnp.max(scores[h], axis=-1, keepdims=True)
+        terms = jnp.exp(scores[h] - highest)
+        total = jnp.sum(terms, axis=-1, keepdims=True)
+        terms_ref[h] = terms
+        tops = jnp.where(lane == 2 * h, highest, jnp.where(lane == 2 * h + 1, total, tops))
+    tops_ref[...] = tops
+
+
 def query_kernel(scale, q_ref, qg_ref, qgain_ref, kgain_ref, bias_ref, *refs):
-    tiles, (qgrad_ref, sums_ref, stats_ref), (keys, values) = refs[:9], refs[9:12], refs[12:]
+    tiles, (near_terms_ref, near_grads_ref, tops_ref, near_keys, near_values) = refs[:3], refs[3:8]
+    qgrad_ref, sums_ref, stats_ref, keys, values = refs[8:]
     _, _, tile, channels = qg_ref.shape
     heads = head_cols(channels)
     fill(tiles, keys, values)
@@ -82,21 +103,31 @@
         dot(qg_ref[0, 0, :, cols], keys[:, cols], NT) * scale + bias_ref[...] for cols in heads
     ]
     prob_grads = [dot(qg_ref[0, 1, :, cols], values[:, cols], NT) for cols in heads]
-    probs = []
+    probs, near_probs = [], []
+    for h in range(len(heads)):
+        near_top = tops_ref[:, 2 * h : 2 * h + 1]
+        highest = jnp.maximum(near_top, jnp.max(scores[h], axis=-1, keepdims=True))
+        terms = jnp.exp(scores[h] - highest)
+        near_scale = jnp.exp(near_top - highest)
+        total = jnp.sum(terms, axis=-1, keepdims=True)
+        total += tops_ref[:, 2 * h + 1 : 2 * h + 2] * near_scale
+        inverse = 1.0 / total
+        probs.append(terms * inverse)
+        near_probs.append(near_terms_ref[h] * (near_scale * inverse))
+        columns = jnp.where(lane == 2 * h, highest + jnp.log(total), columns)
+    outs = []
     for h, cols in enumerate(heads):
-        highest = jnp.max(scores[h], axis=-1, keepdims=True)
-        terms = jnp.exp(scores[h] - highest)
-        total = jnp.sum(terms, axis=-1, keepdims=True)
-        probs.append(terms * (1.0 / total))
-        columns = jnp.where(lane == 2 * h, highest + jnp.log(total), columns)
-    outs = [dot(probs[h].astype(bf16), values[:, cols], NN).astype(bf16) for h, cols in enumerate(heads)]
+        out = dot(near_probs[h].astype(bf16), near_values[:, cols], NN)
+        outs.append((out + dot(probs[h].astype(bf16), values[:, cols], NN)).astype(bf16))
     grads = []
     for h, cols in enumerate(heads):
         products = qg_ref[0, 1, :, cols].astype(f32) * outs[h].astype(f32)
         delta = jnp.sum(products, axis=-1, keepdims=True)
         columns = jnp.where(lane == 2 * h + 1, delta, columns)
         score_grad = (probs[h] * (prob_grads[h] - delta)).astype(bf16)
-        grads.append(dot(score_grad, keys[:, cols], NN) * scale)
+        near_grad = (near_probs[h] * (near_grads_ref[h] - delta)).astype(bf16)
+        grad = dot(near_grad, near_keys[:, cols], NN) + dot(score_grad, keys[:, cols], NN)
+        grads.append(grad * scale)
     for h, cols in enumerate(heads):
         qgrad_ref[:, cols], unit = norm_back(grads[h], q_ref[:, cols], qgain_ref[...])
         qn = qg_ref[0, 0, :, cols].astype(f32)
@@ -107,20 +138,28 @@
     stats_ref[...] = columns.T[:8]
 
 
-def key_kernel(scale, n, bias_ref, *refs):
-    stats, queries_in, keys_in = refs[:3], refs[3:6], refs[6 : 6 + n]
-    outs, (queries, grads, keys, values) = refs[6 + n : -4], refs[-4:]
-    _, _, tile, channels = queries_in[0].shape
-    heads = head_cols(channels)
+def pairs_kernel(scale, bias_ref, *refs):
+    queries_in, keys_in, outs = refs[:3], refs[3:6], refs[6:12]
+    queries, grads, keys, values = outs[4], outs[5], *refs[12:]
+    tile = queries_in[0].shape[2]
     fill(queries_in, queries, grads)
     fill(keys_in, keys, values)
+    near, far = slice(0, 2 * tile), slice(2 * tile, 3 * tile)
+    for h, cols in enumerate(head_cols(queries.shape[1])):
+        for rows, scores_ref, prob_grads_ref in ((near, *outs[:2]), (far, *outs[2:4])):
+            scores = dot(keys[rows, cols], queries[:, cols], NT) * scale
+            scores_ref[h] = scores + bias_ref[...]
+            prob_grads_ref[h] = dot(values[rows, cols], grads[:, cols], NT)
+
+
+def key_kernel(scale, scores_ref, prob_grads_ref, queries, grads, *refs):
+    stats, outs = refs[:3], refs[3:]
+    tile = outs[0].shape[2]
     rows = jnp.concatenate([ref[...] for ref in stats], axis=1)
-    scores = [dot(keys[:, cols], queries[:, cols], NT) * scale for cols in heads]
-    prob_grads = [dot(values[:, cols], grads[:, cols], NT) for cols in heads]
-    for h, cols in enumerate(heads):
-        prob = jnp.exp(scores[h] + (bias_ref[...] - rows[2 * h : 2 * h + 1]))
+    for h, cols in enumerate(head_cols(queries.shape[1])):
+        prob = jnp.exp(scores_ref[h] - rows[2 * h : 2 * h + 1])
         value_terms = dot(prob.astype(bf16), grads[:, cols], NN)
-        score_grad = (prob * (prob_grads[h] - rows[2 * h + 1 : 2 * h + 2])).astype(bf16)
+        score_grad = (prob * (prob_grads_ref[h] - rows[2 * h + 1 : 2 * h + 2])).astype(bf16)
         key_terms = dot(score_grad, queries[:, cols], NN) * scale
         for i, ref in enumerate(outs):
             part = slice(i * tile, (i + 1) * tile)
@@ -128,37 +167,60 @@
             ref[0, 1, :, cols] = value_terms[part].astype(ref.dtype)
 
 
-def query_side(q, qg, qgain, kgain, bias, tiles, scale):
+def near_side(qg, bias, tiles, scale):
     _, _, tile, channels = qg.shape
-    span = len(tiles) * tile
-    qgrad = jax.ShapeDtypeStruct(q.shape, bf16)
-    sums = jax.ShapeDtypeStruct((2, HEAD_DIM), f32)
-    stats = jax.ShapeDtypeStruct((8, tile), f32)
+    span, heads = len(tiles) * tile, channels // HEAD_DIM
+    held = jax.ShapeDtypeStruct((span, channels), bf16)
+    scores = jax.ShapeDtypeStruct((heads, tile, span), f32)
+    return pl.pallas_call(
+        functools.partial(near_kernel, scale),
+        out_shape=[scores, scores, jax.ShapeDtypeStruct((tile, HEAD_DIM), f32), held, held],
+        compiler_params=pltpu.CompilerParams(vmem_limit_bytes=40 * 2**20),
+        cost_estimate=COST,
+        name="near_side",
+    )(qg, bias, *map(in_vmem, tiles))
+
+
+def query_side(q, qg, qgain, kgain, bias, tiles, near, scale):
+    _, _, tile, channels = qg.shape
+    held = pltpu.VMEM((len(tiles) * tile, channels), bf16)
     return pl.pallas_call(
         functools.partial(query_kernel, scale),
-        out_shape=[qgrad, sums, stats],
-        scratch_shapes=[
-            pltpu.VMEM((span, channels), bf16),
-            pltpu.VMEM((span, channels), bf16),
+        out_shape=[
+            jax.ShapeDtypeStruct((tile, channels), bf16),
+            jax.ShapeDtypeStruct((2, HEAD_DIM), f32),
+            jax.ShapeDtypeStruct((8, tile), f32),
         ],
+        scratch_shapes=[held, held],
         compiler_params=pltpu.CompilerParams(vmem_limit_bytes=40 * 2**20),
         cost_estimate=COST,
         name="query_side",
-    )(in_vmem(q), qg, qgain, kgain, bias, *map(in_vmem, tiles))
-
-
-def key_side(bias, stats, queries, keys, types, scale):
-    shape = keys[0].shape
-    _, _, tile, channels = shape
-    held = [pltpu.VMEM((n * tile, channels), bf16) for n in (3, 3, len(keys), len(keys))]
-    return pl.pallas_call(
-        functools.partial(key_kernel, scale, len(keys)),
+    )(in_vmem(q), qg, qgain, kgain, bias, *map(in_vmem, tiles), *map(in_vmem, near))
+
+
+def pairs_side(bias, queries, keys, scale):
+    _, _, tile, channels = keys[0].shape
+    span, heads = 3 * tile, channels // HEAD_DIM
+    shapes = [jax.ShapeDtypeStruct((heads, n * tile, span), f32) for n in (2, 2, 1, 1)]
+    held = [jax.ShapeDtypeStruct((span, channels), bf16)] * 2
+    return pl.pallas_call(
+        functools.partial(pairs_kernel, scale),
+        out_shape=shapes + held,
+        scratch_shapes=[pltpu.VMEM((span, channels), bf16)] * 2,
+        compiler_params=pltpu.CompilerParams(vmem_limit_bytes=40 * 2**20),
+        cost_estimate=COST,
+        name="pairs_side",
+    )(bias, *map(in_vmem, queries), *map(in_vmem, keys))
+
+
+def key_side(stats, scores, prob_grads, queries, grads, shape, types, scale):
+    return pl.pallas_call(
+        functools.partial(key_kernel, scale),
         out_shape=[jax.ShapeDtypeStruct(shape, t) for t in types],
-        scratch_shapes=held,
         compiler_params=pltpu.CompilerParams(vmem_limit_bytes=40 * 2**20),
         cost_estimate=COST,
         name="key_side",
-    )(bias, *stats, *map(in_vmem, queries), *keys)
+    )(*map(in_vmem, (scores, prob_grads, queries, grads)), *stats)
 
 
 def finish_kernel(factor, k_ref, gain_ref, own_ref, mate_ref, sums_ref, *outs):
@@ -259,12 +321,11 @@
     return (at == 0) | (at == n - 1)
 
 
-def mask_bias(tile, rows):
-    each = 3 if rows else 1
-    slot = lax.broadcasted_iota(jnp.int32, (1, 3 * each * tile), 1) // tile
-    gone = outside("tm") & (slot >= 2 * each)
-    if rows:
-        gone |= outside("height") & (slot % 3 == 2)
+def mask_bias(tile, tiles, far_from, beyond):
+    slot = lax.broadcasted_iota(jnp.int32, (1, tiles * tile), 1) // tile
+    gone = outside("tm") & (slot >= far_from)
+    if beyond:
+        gone |= outside("height")
     return jnp.where(gone, MASKED, 0.0).astype(f32)
 
 
@@ -288,21 +349,25 @@
     c0, d0, y0, w0 = together(frames, lambda a, b: (a, b, a, b), kv, qg)
     z, c0, d0, y0, w0 = lax.optimization_barrier((z, c0, d0, y0, w0))
     c1 = swap(z, "tm")
-    x, y1 = hop(z), far(z)
-    x, y1, c1 = lax.optimization_barrier((x, y1, c1))
+    y1, x = far(z), hop(z)
+    y1, c1, x = lax.optimization_barrier((y1, c1, x))
     y2, c2 = far(x), swap(x, "tm")
-    tiles = [kv, z, x, c0, c1, c2, y0, y1, y2]
+    near = near_side(qg, mask_bias(tile, 6, 4, False), [kv, z, c0, c1, y0, y1], scale)
+    pairs = pairs_side(mask_bias(tile, 3, 2, False), [qg, d0, w0], [kv, z, x], scale)
+    near, pairs = lax.optimization_barrier((near, pairs))
+    far_bias = mask_bias(tile, 3, 2, True)
     q_out, sums, stats = query_side(
-        q_flat, qg, qg_gain, kg_gain, mask_bias(tile, True), tiles, scale
+        q_flat, qg, qg_gain, kg_gain, far_bias, [x, c2, y2], near, scale
     )
 
     c_stats = swap(with_sums(stats, sums), "tm")
     sums = sums + c_stats[6:8, :HEAD_DIM]
     y_stats = far(stats)
     sums = level(sums, "heads", "heads", 1, 2)
-    near = mask_bias(tile, False), [stats, c_stats, y_stats], [qg, d0, w0]
-    (px,) = key_side(*near, [x], [bf16], scale)
-    own, pz = key_side(*near, [kv, z], [f32, bf16], scale)
+    stats = [stats, c_stats, y_stats]
+    near_pairs, far_pairs, held = pairs[:2], pairs[2:4], pairs[4:]
+    (px,) = key_side(stats, *far_pairs, *held, kv.shape, [bf16], scale)
+    own, pz = key_side(stats, *near_pairs, *held, kv.shape, [f32, bf16], scale)
     px, sums = lax.optimization_barrier((px, sums))
     pz = plus(pz, hop(px, True))
     sums = sums + swap(sums, "height")

time: 89.4 us -> 87.9 us (0.983)
  the two profiles are of different devices: /device:TPU:1 before, /device:TPU:32 now
where the time goes in v1:
time: 87.9 us; the launch traced here: 87.5 us
  starting transfers between devices  37.9 us (43%)
  waiting for transfers between devices  16.5 us (19%)
  blocking collectives  15.8 us (18%)
  Pallas kernels  15.6 us (18%)
    ppermute x11, starting transfers between devices, swapped(): return lax.ppermute(x, axis, [(i, i ^ bits) for i in range(n)])  28.2 us
    all_to_all x1, blocking collectives, last_levels(): got = lax.all_to_all(sent, ('tm', 'height'), 0, 0, axis_index_groups=groups)  15.8 us
    ppermute x2, waiting for transfers between devices, hop(): return lax.ppermute(x, 'height', rows_route(lax.axis_size('height'), back))  8.47 us
    ppermute x11, waiting for transfers between devices, swapped(): return lax.ppermute(x, axis, [(i, i ^ bits) for i in range(n)])  8.02 us
    ppermute x5, starting transfers between devices, far(): return lax.ppermute(x, 'tm', frames_route(lax.axis_size('tm')))  4.9 us
    ppermute x2, starting transfers between devices, hop(): return lax.ppermute(x, 'height', rows_route(lax.axis_size('height'), back))  4.81 us
    pallas_call x1, Pallas kernels, query_side(): pl.pallas_call(functools.partial(query_kernel, scale), out_shape=[jax.Sha...  3.94 us
    pallas_call x2, Pallas kernels, norm_stack(): pl.pallas_call(stack_kernel, out_shape=[jax.ShapeDtypeStruct((1, 2, token...  3.32 us
  transfers between devices with their start and end apart: 18, of which 8 were waited for; matrix products, arithmetic and copies ran while one was open for 1% of the time, Pallas kernels for 10%

profile of v1, /device:TPU:32, one launch (start us, length us, event | category | flops | bytes accessed | tf_op | source)
XLA Modules:
  0.0 87.5 jit_solution(3903314372837006258)
XLA Ops:
  1.9 6.4 %collective-permute-start.4 = (bf16[1,2,192,384]{3,2,1,0:T(8,128)(2,1)S(1)}, bf16[1,2,192,384]{3,2,1,0:T(8,128)(2,1)S(1)}, u32[]{:S(2)}, u32[]{:S(2)}) collective-permute-start(bf16[1,2,192,384]{3,2,1,0:T(8,128)(2,1)S(1)} %norm_stack.3.refs_0_.refs_3_), channel_id=1, source_target_pairs={{0,4},{4,0},{8,12},{12,8},{16,20},{20,16},{24,28},{28,24},{1,5},{5... | collective-permute-start | bytes 884744 | tf_op jit(solution)/shard_map/ppermute | solution.py:254
  8.2 2.1 %norm_stack.2 = (bf16[1,2,192,384]{3,2,1,0:T(8,128)(2,1)S(1)}, bf16[192,384]{1,0:T(8,128)(2,1)}, bf16[192,384]{1,0:T(8,128)(2,1)}) custom-call(bf16[6,8,4,384]{3,2,1,0:T(4,128)(2,1)} %refs_0_.1, bf16[6,8,4,384]{3,2,1,0:T(4,128)(2,1)} %other_ref.2, f32[1,128]{1,0:T(1,128)} %bitcast.7, bf16[6,8,4,384]{3,2,1,0:T(4,128)(2,1)} %refs_0_.1, ...), custom_call_target="tpu_custom_call" | custom-call | flops 1000000 | bytes 100000 | tf_op jit(solution)/shard_map/norm_stack/pallas_call | solution.py:49
  10.3 8.9 %conditional.2 = (bf16[1,2,192,384]{3,2,1,0:T(8,128)(2,1)}, bf16[1,2,192,384]{3,2,1,0:T(8,128)(2,1)}, bf16[1,2,192,384]{3,2,1,0:T(8,128)(2,1)}, bf16[1,2,192,384]{3,2,1,0:T(8,128)(2,1)}) conditional(s32[]{:T(128)} %convert_element_type.13, (bf16[1,2,192,384]{3,2,1,0:T(8,128)(2,1)S(1)}, bf16[1,2,192,384]{3,2,1,0:T(8,128)(2,1)S(1)}) %tuple.31, ...), branch_computations={%region_0.0_spmd, %region_1.0_spmd} | conditional | bytes 4718784 | solution.py:292
  10.3 1.5 %collective-permute-start.2 = (bf16[1,2,192,384]{3,2,1,0:T(8,128)(2,1)S(1)}, bf16[1,2,192,384]{3,2,1,0:T(8,128)(2,1)}, u32[]{:S(2)}, u32[]{:S(2)}) collective-permute-start(bf16[1,2,192,384]{3,2,1,0:T(8,128)(2,1)S(1)} %get-tuple-element.27), channel_id=1, source_target_pairs={{32,64},{64,32},{96,128},{128,96},{160,192},{192,160},{33,65},{65,... | collective-permute-start | bytes 884744 | tf_op jit(solution)/shard_map/cond/branch_1_fun/ppermute | solution.py:275
  11.9 2.3 %collective-permute-start = (bf16[1,2,192,384]{3,2,1,0:T(8,128)(2,1)S(1)}, bf16[1,2,192,384]{3,2,1,0:T(8,128)(2,1)}, u32[]{:S(2)}, u32[]{:S(2)}) collective-permute-start(bf16[1,2,192,384]{3,2,1,0:T(8,128)(2,1)S(1)} %get-tuple-element.27), channel_id=1, source_target_pairs={{0,32},{32,0},{64,96},{96,64},{128,160},{160,128},{192,224},{224,1... | collective-permute-start | bytes 884744 | tf_op jit(solution)/shard_map/cond/branch_1_fun/ppermute | solution.py:254
  14.2 1.4 %collective-permute-start.3 = (bf16[1,2,192,384]{3,2,1,0:T(8,128)(2,1)S(1)}, bf16[1,2,192,384]{3,2,1,0:T(8,128)(2,1)}, u32[]{:S(2)}, u32[]{:S(2)}) collective-permute-start(bf16[1,2,192,384]{3,2,1,0:T(8,128)(2,1)S(1)} %get-tuple-element.28), channel_id=1, source_target_pairs={{32,64},{64,32},{96,128},{128,96},{160,192},{192,160},{33,65},{65,... | collective-permute-start | bytes 884744 | tf_op jit(solution)/shard_map/cond/branch_1_fun/ppermute | solution.py:275
  15.6 2.3 %collective-permute-start.1 = (bf16[1,2,192,384]{3,2,1,0:T(8,128)(2,1)S(1)}, bf16[1,2,192,384]{3,2,1,0:T(8,128)(2,1)}, u32[]{:S(2)}, u32[]{:S(2)}) collective-permute-start(bf16[1,2,192,384]{3,2,1,0:T(8,128)(2,1)S(1)} %get-tuple-element.28), channel_id=1, source_target_pairs={{0,32},{32,0},{64,96},{96,64},{128,160},{160,128},{192,224},{224,1... | collective-permute-start | bytes 884744 | tf_op jit(solution)/shard_map/cond/branch_1_fun/ppermute | solution.py:254
  17.9 1.3 %collective-permute-done.1 = bf16[1,2,192,384]{3,2,1,0:T(8,128)(2,1)} collective-permute-done((bf16[1,2,192,384]{3,2,1,0:T(8,128)(2,1)S(1)}, bf16[1,2,192,384]{3,2,1,0:T(8,128)(2,1)}, u32[]{:S(2)}, u32[]{:S(2)}) %collective-permute-start.1) | collective-permute-done | bytes 294944 | tf_op jit(solution)/shard_map/cond/branch_1_fun/ppermute | solution.py:254
  19.2 2.4 %collective-permute-done.4.refs_1_.refs_4_ = bf16[1,2,192,384]{3,2,1,0:T(8,128)(2,1)S(1)} collective-permute-done((bf16[1,2,192,384]{3,2,1,0:T(8,128)(2,1)S(1)}, bf16[1,2,192,384]{3,2,1,0:T(8,128)(2,1)S(1)}, u32[]{:S(2)}, u32[]{:S(2)}) %collective-permute-start.4) | collective-permute-done | bytes 294944 | tf_op jit(solution)/shard_map/ppermute | solution.py:254
  21.6 3.4 %collective-permute-start.7 = (bf16[1,2,192,384]{3,2,1,0:T(8,128)(2,1)S(1)}, bf16[1,2,192,384]{3,2,1,0:T(8,128)(2,1)S(1)}, u32[]{:S(2)}, u32[]{:S(2)}) collective-permute-start(bf16[1,2,192,384]{3,2,1,0:T(8,128)(2,1)S(1)} %collective-permute-done.4.refs_1_.refs_4_), channel_id=1, source_target_pairs={{0,8},{8,16},{12,4},{16,24},{20,12},{28,20},{1,9},{9,17},{13,5},{1... | collective-permute-start | bytes 884744 | tf_op jit(solution)/shard_map/ppermute | solution.py:271
  26.3 5.9 %collective-permute-done.7.refs_5_.refs_0_ = bf16[1,2,192,384]{3,2,1,0:T(8,128)(2,1)S(1)} collective-permute-done((bf16[1,2,192,384]{3,2,1,0:T(8,128)(2,1)S(1)}, bf16[1,2,192,384]{3,2,1,0:T(8,128)(2,1)S(1)}, u32[]{:S(2)}, u32[]{:S(2)}) %collective-permute-start.7) | collective-permute-done | bytes 294944 | tf_op jit(solution)/shard_map/ppermute | solution.py:271
  32.8 4.7 %collective-permute-start.8 = (bf16[1,2,192,384]{3,2,1,0:T(8,128)(2,1)S(1)}, bf16[1,2,192,384]{3,2,1,0:T(8,128)(2,1)S(1)}, u32[]{:S(2)}, u32[]{:S(2)}) collective-permute-start(bf16[1,2,192,384]{3,2,1,0:T(8,128)(2,1)S(1)} %collective-permute-done.7.refs_5_.refs_0_), channel_id=1, source_target_pairs={{0,32},{32,0},{64,96},{96,64},{128,160},{160,128},{192,224},{224,1... | collective-permute-start | bytes 884744 | tf_op jit(solution)/shard_map/ppermute | solution.py:254
  37.6 2.4 %pairs_side.1 = (f32[3,384,576]{2,1,0:T(8,128)S(1)}, f32[3,384,576]{2,1,0:T(8,128)S(1)}, f32[3,192,576]{2,1,0:T(8,128)S(1)}, f32[3,192,576]{2,1,0:T(8,128)S(1)},...) custom-call(f32[1,576]{1,0:T(1,128)S(1)} %broadcast_select_fusion.bias_ref, ...), custom_call_target="tpu_custom_call" | custom-call | flops 1000000 | bytes 100000 | tf_op jit(solution)/shard_map/pairs_side/pallas_call | solution.py:206
  40.0 2.5 %near_side.1 = (f32[3,192,1152]{2,1,0:T(8,128)S(1)}, f32[3,192,1152]{2,1,0:T(8,128)S(1)}, f32[192,128]{1,0:T(8,128)S(1)}, bf16[1152,384]{1,0:T(8,128)(2,1)S(1)}, bf16[1152,384]{1,0:T(8,128)(2,1)S(1)}) custom-call(bf16[1,2,192,384]{3,2,1,0:T(8,128)(2,1)S(1)} %get-tuple-element.85.qg_ref.refs_0_, f32[1,1152]{1,0:T(1,128)S(1)} %and_select_fusion.bias_ref, ...), custom_call_target="tpu_custom_call" | custom-call | flops 1000000 | bytes 100000 | tf_op jit(solution)/shard_map/near_side/pallas_call | solution.py:175
  42.6 3.9 %query_side.1 = (bf16[192,384]{1,0:T(8,128)(2,1)S(1)}, f32[2,128]{1,0:T(2,128)S(1)}, f32[8,192]{1,0:T(8,128)S(1)}) custom-call(bf16[192,384]{1,0:T(8,128)(2,1)S(1)} %copy-done.1, bf16[1,2,192,384]{3,2,1,0:T(8,128)(2,1)S(1)} %get-tuple-element.85.qg_ref.refs_0_, f32[1,128]{1,0:T(1,128)S(1)} %bitcast.8, f32[1,128]{1,0:T(1,128)S(1)} %bitcast.6, ...), custom_call_target="tpu_custom_call" | custom-call | flops 1000000 | bytes 100000 | tf_op jit(solution)/shard_map/query_side/pallas_call | solution.py:187
  48.8 2.4 %collective-permute-start.13 = (f32[2,128]{1,0:T(2,128)S(1)}, f32[2,128]{1,0:T(2,128)S(1)}, u32[]{:S(2)}, u32[]{:S(2)}) collective-permute-start(f32[2,128]{1,0:T(2,128)S(1)} %slice_add_fusion), channel_id=1, source_target_pairs={{0,2},{1,3},{2,0},{3,1},{4,6},{5,7},{6,4},{7,5},{8,10},{9,11},{10,... | collective-permute-start | bytes 3080 | tf_op jit(solution)/shard_map/ppermute | solution.py:254
  53.3 1.5 %collective-permute-done.12 = f32[2,128]{1,0:T(2,128)S(1)} collective-permute-done((f32[2,128]{1,0:T(2,128)S(1)}, f32[2,128]{1,0:T(2,128)S(1)}, u32[]{:S(2)}, u32[]{:S(2)}) %collective-permute-start.12) | collective-permute-done | bytes 1056 | tf_op jit(solution)/shard_map/ppermute | solution.py:254
  54.8 1.4 %collective-permute-start.15 = (bf16[1,2,192,384]{3,2,1,0:T(8,128)(2,1)S(1)}, bf16[1,2,192,384]{3,2,1,0:T(8,128)(2,1)S(1)}, u32[]{:S(2)}, u32[]{:S(2)}) collective-permute-start(bf16[1,2,192,384]{3,2,1,0:T(8,128)(2,1)S(1)} %key_side.3), channel_id=1, source_target_pairs={{8,0},{16,8},{4,12},{24,16},{12,20},{20,28},{9,1},{17,9},{5,13},{2... | collective-permute-start | bytes 884744 | tf_op jit(solution)/shard_map/ppermute | solution.py:271
  56.2 5.5 %collective-permute-start.16 = (f32[2,128]{1,0:T(2,128)S(1)}, f32[2,128]{1,0:T(2,128)S(1)}, u32[]{:S(2)}, u32[]{:S(2)}) collective-permute-start(f32[2,128]{1,0:T(2,128)S(1)} %add_add_fusion), channel_id=1, source_target_pairs={{0,4},{4,0},{8,12},{12,8},{16,20},{20,16},{24,28},{28,24},{1,5},{5... | collective-permute-start | bytes 3080 | tf_op jit(solution)/shard_map/ppermute | solution.py:254
  63.7 2.6 %collective-permute-done.15 = bf16[1,2,192,384]{3,2,1,0:T(8,128)(2,1)S(1)} collective-permute-done((bf16[1,2,192,384]{3,2,1,0:T(8,128)(2,1)S(1)}, bf16[1,2,192,384]{3,2,1,0:T(8,128)(2,1)S(1)}, u32[]{:S(2)}, u32[]{:S(2)}) %collective-permute-start.15) | collective-permute-done | bytes 294944 | tf_op jit(solution)/shard_map/ppermute | solution.py:271
  66.4 2.9 %collective-permute-start.17 = (bf16[1,2,192,384]{3,2,1,0:T(8,128)(2,1)S(1)}, bf16[1,2,192,384]{3,2,1,0:T(8,128)(2,1)S(1)}, u32[]{:S(2)}, u32[]{:S(2)}) collective-permute-start(bf16[1,2,192,384]{3,2,1,0:T(8,128)(2,1)S(1)} %add_convert_fusion), channel_id=1, source_target_pairs={{0,4},{4,0},{8,12},{12,8},{16,20},{20,16},{24,28},{28,24},{1,5},{5... | collective-permute-start | bytes 884744 | tf_op jit(solution)/shard_map/ppermute | solution.py:254
  70.0 15.8 %conditional.3 = (f32[2,128]{1,0:T(2,128)S(1)}) conditional(s32[]{:T(128)} %convert_element_type.13, f32[2,128]{1,0:T(2,128)S(1)} %add.47, f32[2,128]{1,0:T(2,128)S(1)} %add.47), branch_computations={%region_2.3_spmd, %region_3.5_spmd} | conditional | flops 3840 | bytes 67596 | solution.py:292
  70.0 15.8 %all_to_all.4 = f32[16,2,128]{2,1,0:T(2,128)S(1)} all-to-all(f32[16,2,128]{2,1,0:T(2,128)S(1)} %broadcast_in_dim.19), channel_id=1, replica_groups={{0,8,16,24,64,72,80,88,128,136,144,152,192,200,208,216},{4,12,20,28,68,..., dimensions={0} | all-to-all | bytes 32768 | tf_op jit(solution)/shard_map/cond/branch_1_fun/all_to_all | solution.py:307
  85.9 1.7 %finish.1 = (bf16[6,8,4,384]{3,2,1,0:T(4,128)(2,1)}, bf16[6,8,4,384]{3,2,1,0:T(4,128)(2,1)}, f32[1,128]{1,0:T(1,128)}, f32[1,128]{1,0:T(1,128)}) custom-call(bf16[192,384]{1,0:T(8,128)(2,1)S(1)} %copy-done, f32[1,128]{1,0:T(1,128)} %bitcast.5, f32[1,2,192,384]{3,2,1,0:T(8,128)S(1)} %get-tuple-element.122.own_ref, ...), custom_call_target="tpu_custom_call" | custom-call | flops 1000000 | bytes 100000 | tf_op jit(solution)/shard_map/finish/pallas_call | solution.py:240
  (43 shorter events, 10.4 us)
Async XLA Ops:
  1.9 19.8 %collective-permute-start.4 = (bf16[1,2,192,384]{3,2,1,0:T(8,128)(2,1)S(1)}, bf16[1,2,192,384]{3,2,1,0:T(8,128)(2,1)S(1)}, u32[]{:S(2)}, u32[]{:S(2)}) collective-permute-start(bf16[1,2,192,384]{3,2,1,0:T(8,128)(2,1)S(1)} %norm_stack.3.refs_0_.refs_3_), channel_id=1, source_target_pairs={{0,4},{4,0},{8,12},{12,8},{16,20},{20,16},{24,28},{28,24},{1,5},{5... | collective-permute-start | bytes 884744 | tf_op jit(solution)/shard_map/ppermute | solution.py:254
  10.3 32.2 %copy-start.1 = (bf16[192,384]{1,0:T(8,128)(2,1)S(1)}, bf16[192,384]{1,0:T(8,128)(2,1)}, u32[]{:S(2)}) copy-start(bf16[192,384]{1,0:T(8,128)(2,1)} %get-tuple-element.84.q_ref) | copy-start | bytes 442372
  10.3 32.2 %copy-start.2 = (f32[128]{0:T(128)S(1)}, f32[128]{0:T(128)}, u32[]{:S(2)}) copy-start(f32[128]{0:T(128)} %param.17) | copy-start | bytes 1540
  10.3 32.2 %copy-start.3 = (f32[128]{0:T(128)S(1)}, f32[128]{0:T(128)}, u32[]{:S(2)}) copy-start(f32[128]{0:T(128)} %param.16) | copy-start | bytes 1540
  10.3 7.5 %collective-permute-start.2 = (bf16[1,2,192,384]{3,2,1,0:T(8,128)(2,1)S(1)}, bf16[1,2,192,384]{3,2,1,0:T(8,128)(2,1)}, u32[]{:S(2)}, u32[]{:S(2)}) collective-permute-start(bf16[1,2,192,384]{3,2,1,0:T(8,128)(2,1)S(1)} %get-tuple-element.27), channel_id=1, source_target_pairs={{32,64},{64,32},{96,128},{128,96},{160,192},{192,160},{33,65},{65,... | collective-permute-start | bytes 884744 | tf_op jit(solution)/shard_map/cond/branch_1_fun/ppermute | solution.py:275
  11.9 6.0 %collective-permute-start = (bf16[1,2,192,384]{3,2,1,0:T(8,128)(2,1)S(1)}, bf16[1,2,192,384]{3,2,1,0:T(8,128)(2,1)}, u32[]{:S(2)}, u32[]{:S(2)}) collective-permute-start(bf16[1,2,192,384]{3,2,1,0:T(8,128)(2,1)S(1)} %get-tuple-element.27), channel_id=1, source_target_pairs={{0,32},{32,0},{64,96},{96,64},{128,160},{160,128},{192,224},{224,1... | collective-permute-start | bytes 884744 | tf_op jit(solution)/shard_map/cond/branch_1_fun/ppermute | solution.py:254
  14.2 3.7 %collective-permute-start.3 = (bf16[1,2,192,384]{3,2,1,0:T(8,128)(2,1)S(1)}, bf16[1,2,192,384]{3,2,1,0:T(8,128)(2,1)}, u32[]{:S(2)}, u32[]{:S(2)}) collective-permute-start(bf16[1,2,192,384]{3,2,1,0:T(8,128)(2,1)S(1)} %get-tuple-element.28), channel_id=1, source_target_pairs={{32,64},{64,32},{96,128},{128,96},{160,192},{192,160},{33,65},{65,... | collective-permute-start | bytes 884744 | tf_op jit(solution)/shard_map/cond/branch_1_fun/ppermute | solution.py:275
  15.6 3.6 %collective-permute-start.1 = (bf16[1,2,192,384]{3,2,1,0:T(8,128)(2,1)S(1)}, bf16[1,2,192,384]{3,2,1,0:T(8,128)(2,1)}, u32[]{:S(2)}, u32[]{:S(2)}) collective-permute-start(bf16[1,2,192,384]{3,2,1,0:T(8,128)(2,1)S(1)} %get-tuple-element.28), channel_id=1, source_target_pairs={{0,32},{32,0},{64,96},{96,64},{128,160},{160,128},{192,224},{224,1... | collective-permute-start | bytes 884744 | tf_op jit(solution)/shard_map/cond/branch_1_fun/ppermute | solution.py:254
  21.6 10.5 %collective-permute-start.7 = (bf16[1,2,192,384]{3,2,1,0:T(8,128)(2,1)S(1)}, bf16[1,2,192,384]{3,2,1,0:T(8,128)(2,1)S(1)}, u32[]{:S(2)}, u32[]{:S(2)}) collective-permute-start(bf16[1,2,192,384]{3,2,1,0:T(8,128)(2,1)S(1)} %collective-permute-done.4.refs_1_.refs_4_), channel_id=1, source_target_pairs={{0,8},{8,16},{12,4},{16,24},{20,12},{28,20},{1,9},{9,17},{13,5},{1... | collective-permute-start | bytes 884744 | tf_op jit(solution)/shard_map/ppermute | solution.py:271
  25.1 7.1 %collective-permute-start.6 = (bf16[1,2,192,384]{3,2,1,0:T(8,128)(2,1)S(1)}, bf16[1,2,192,384]{3,2,1,0:T(8,128)(2,1)S(1)}, u32[]{:S(2)}, u32[]{:S(2)}) collective-permute-start(bf16[1,2,192,384]{3,2,1,0:T(8,128)(2,1)S(1)} %collective-permute-done.4.refs_1_.refs_4_), channel_id=1, source_target_pairs={{0,32},{32,0},{64,96},{96,64},{128,160},{160,128},{192,224},{224,1... | collective-permute-start | bytes 884744 | tf_op jit(solution)/shard_map/ppermute | solution.py:254
  25.6 6.6 %collective-permute-start.5 = (bf16[1,2,192,384]{3,2,1,0:T(8,128)(2,1)S(1)}, bf16[1,2,192,384]{3,2,1,0:T(8,128)(2,1)S(1)}, u32[]{:S(2)}, u32[]{:S(2)}) collective-permute-start(bf16[1,2,192,384]{3,2,1,0:T(8,128)(2,1)S(1)} %collective-permute-done.4.refs_1_.refs_4_), channel_id=1, source_target_pairs={{32,64},{64,32},{96,128},{128,96},{160,192},{192,160},{33,65},{65,... | collective-permute-start | bytes 884744 | tf_op jit(solution)/shard_map/ppermute | solution.py:275
  32.2 10.4 %collective-permute-start.9 = (bf16[1,2,192,384]{3,2,1,0:T(8,128)(2,1)S(1)}, bf16[1,2,192,384]{3,2,1,0:T(8,128)(2,1)S(1)}, u32[]{:S(2)}, u32[]{:S(2)}) collective-permute-start(bf16[1,2,192,384]{3,2,1,0:T(8,128)(2,1)S(1)} %collective-permute-done.7.refs_5_.refs_0_), channel_id=1, source_target_pairs={{32,64},{64,32},{96,128},{128,96},{160,192},{192,160},{33,65},{65,... | collective-permute-start | bytes 884744 | tf_op jit(solution)/shard_map/ppermute | solution.py:275
  32.8 9.7 %collective-permute-start.8 = (bf16[1,2,192,384]{3,2,1,0:T(8,128)(2,1)S(1)}, bf16[1,2,192,384]{3,2,1,0:T(8,128)(2,1)S(1)}, u32[]{:S(2)}, u32[]{:S(2)}) collective-permute-start(bf16[1,2,192,384]{3,2,1,0:T(8,128)(2,1)S(1)} %collective-permute-done.7.refs_5_.refs_0_), channel_id=1, source_target_pairs={{0,32},{32,0},{64,96},{96,64},{128,160},{160,128},{192,224},{224,1... | collective-permute-start | bytes 884744 | tf_op jit(solution)/shard_map/ppermute | solution.py:254
  46.5 1.3 %collective-permute-start.10 = (f32[8,192]{1,0:T(8,128)S(1)}, f32[8,192]{1,0:T(8,128)S(1)}, u32[]{:S(2)}, u32[]{:S(2)}) collective-permute-start(f32[8,192]{1,0:T(8,128)S(1)} %constant_dynamic-update-slice_fusion), channel_id=1, source_target_pairs={{0,32},{32,0},{64,96},{96,64},{128,160},{160,128},{192,224},{224,1... | collective-permute-start | bytes 18440 | tf_op jit(solution)/shard_map/ppermute | solution.py:254
  46.6 4.7 %collective-permute-start.11 = (f32[8,192]{1,0:T(8,128)S(1)}, f32[8,192]{1,0:T(8,128)S(1)}, u32[]{:S(2)}, u32[]{:S(2)}) collective-permute-start(f32[8,192]{1,0:T(8,128)S(1)} %get-tuple-element.120.refs_0_), channel_id=1, source_target_pairs={{32,64},{64,32},{96,128},{128,96},{160,192},{192,160},{33,65},{65,... | collective-permute-start | bytes 18440 | tf_op jit(solution)/shard_map/ppermute | solution.py:275
  47.8 4.2 %collective-permute-start.14 = (f32[2,128]{1,0:T(2,128)S(1)}, f32[2,128]{1,0:T(2,128)S(1)}, u32[]{:S(2)}, u32[]{:S(2)}) collective-permute-start(f32[2,128]{1,0:T(2,128)S(1)} %slice_add_fusion), channel_id=1, source_target_pairs={{0,3},{1,2},{2,1},{3,0},{4,7},{5,6},{6,5},{7,4},{8,11},{9,10},{10,... | collective-permute-start | bytes 3080 | tf_op jit(solution)/shard_map/ppermute | solution.py:254
  48.8 4.5 %collective-permute-start.13 = (f32[2,128]{1,0:T(2,128)S(1)}, f32[2,128]{1,0:T(2,128)S(1)}, u32[]{:S(2)}, u32[]{:S(2)}) collective-permute-start(f32[2,128]{1,0:T(2,128)S(1)} %slice_add_fusion), channel_id=1, source_target_pairs={{0,2},{1,3},{2,0},{3,1},{4,6},{5,7},{6,4},{7,5},{8,10},{9,11},{10,... | collective-permute-start | bytes 3080 | tf_op jit(solution)/shard_map/ppermute | solution.py:254
  51.2 3.6 %collective-permute-start.12 = (f32[2,128]{1,0:T(2,128)S(1)}, f32[2,128]{1,0:T(2,128)S(1)}, u32[]{:S(2)}, u32[]{:S(2)}) collective-permute-start(f32[2,128]{1,0:T(2,128)S(1)} %slice_add_fusion), channel_id=1, source_target_pairs={{0,1},{1,0},{2,3},{3,2},{4,5},{5,4},{6,7},{7,6},{8,9},{9,8},{10,11... | collective-permute-start | bytes 3080 | tf_op jit(solution)/shard_map/ppermute | solution.py:254
  54.8 31.1 %copy-start = (bf16[192,384]{1,0:T(8,128)(2,1)S(1)}, bf16[192,384]{1,0:T(8,128)(2,1)}, u32[]{:S(2)}) copy-start(bf16[192,384]{1,0:T(8,128)(2,1)} %get-tuple-element.115.k_ref) | copy-start | bytes 442372
  54.8 11.6 %collective-permute-start.15 = (bf16[1,2,192,384]{3,2,1,0:T(8,128)(2,1)S(1)}, bf16[1,2,192,384]{3,2,1,0:T(8,128)(2,1)S(1)}, u32[]{:S(2)}, u32[]{:S(2)}) collective-permute-start(bf16[1,2,192,384]{3,2,1,0:T(8,128)(2,1)S(1)} %key_side.3), channel_id=1, source_target_pairs={{8,0},{16,8},{4,12},{24,16},{12,20},{20,28},{9,1},{17,9},{5,13},{2... | collective-permute-start | bytes 884744 | tf_op jit(solution)/shard_map/ppermute | solution.py:271
  56.2 7.6 %collective-permute-start.16 = (f32[2,128]{1,0:T(2,128)S(1)}, f32[2,128]{1,0:T(2,128)S(1)}, u32[]{:S(2)}, u32[]{:S(2)}) collective-permute-start(f32[2,128]{1,0:T(2,128)S(1)} %add_add_fusion), channel_id=1, source_target_pairs={{0,4},{4,0},{8,12},{12,8},{16,20},{20,16},{24,28},{28,24},{1,5},{5... | collective-permute-start | bytes 3080 | tf_op jit(solution)/shard_map/ppermute | solution.py:254
  66.4 19.4 %collective-permute-start.17 = (bf16[1,2,192,384]{3,2,1,0:T(8,128)(2,1)S(1)}, bf16[1,2,192,384]{3,2,1,0:T(8,128)(2,1)S(1)}, u32[]{:S(2)}, u32[]{:S(2)}) collective-permute-start(bf16[1,2,192,384]{3,2,1,0:T(8,128)(2,1)S(1)} %add_convert_fusion), channel_id=1, source_target_pairs={{0,4},{4,0},{8,12},{12,8},{16,20},{20,16},{24,28},{28,24},{1,5},{5... | collective-permute-start | bytes 884744 | tf_op jit(solution)/shard_map/ppermute | solution.py:254
